TPU v7x, 32 devices: a whole 2x2x4 slice. The times are simulated.
32 devices in a mesh: lat: 8 (over z, x), lon: 4 (over y, core).
Axes of the slice: x: 2, y: 2, z: 4, core: 2. Of those that a mesh axis runs over, the one named last changes fastest.
Arguments:
- stream: bfloat16 [128, 1024, 256], P('lat', 'lon'), may hold values from -6 to 6
- cotangent: bfloat16 [128, 1024, 256], P('lat', 'lon'), may hold values from -6 to 6
- w_expand: bfloat16 [256, 512], replicated, may hold values from -0.375 to 0.375
- w_reduce: bfloat16 [512, 256], replicated, may hold values from -0.25 to 0.25
- legendre: bfloat16 [512, 128, 512], P(('lat', 'lon')), as said below
- quadrature: float32 [128], replicated, may hold values from 0.2 to 2
- spectral_mix: bfloat16 [512, 256, 256], P(('lat', 'lon')), may hold values from -0.375 to 0.375
Outputs:
- grad_input: bfloat16 [128, 1024, 256], P('lat', 'lon')
- grad_expand: float32 [256, 512], replicated
- grad_reduce: float32 [512, 256], replicated
Inputs may be any that keep to these rules, and one draw needn't show every extreme that they name: legendre[m, a, l] is zero wherever l < m.
All inputs are finite; a program needn't handle non-finite values.
Results may differ from a plain program's by a relative error of at most 0.009.
Values may be sent and summed in bfloat16 or wider, within the bound.
A program may use at most 128 MiB of HBM per device.

v0:
```python
import math

import jax
import jax.numpy as jnp
from jax import lax
from jax.sharding import PartitionSpec as P


def gelu_value(preact):
    inside = 0.7978845608028654 * (preact + 0.044715 * preact * preact * preact)
    return 0.5 * preact * (1.0 + jnp.tanh(inside))


def gelu_slope(preact):
    inside = 0.7978845608028654 * (preact + 0.044715 * preact * preact * preact)
    tanh_val = jnp.tanh(inside)
    return 0.5 * (1.0 + tanh_val) + 0.5 * preact * (
        1.0 - tanh_val * tanh_val
    ) * 0.7978845608028654 * (1.0 + 3.0 * 0.044715 * preact * preact)


def dft_table(count, order_count):
    lon_index = jnp.arange(count, dtype=jnp.int32)[:, None]
    order_index = jnp.arange(order_count, dtype=jnp.int32)[None, :]
    angles = (lon_index * order_index % count).astype(jnp.float32) * (2.0 * math.pi / count)
    factor = 1.0 / math.sqrt(count)
    return jnp.stack([jnp.cos(angles) * factor, -jnp.sin(angles) * factor]).astype(jnp.bfloat16)


def on_device(stream, cotangent, w_expand, w_reduce, legendre, quadrature, spectral_mix):
    lat_count = lax.axis_size("lat")
    lon_count = lax.axis_size("lon")
    rows_here = stream.shape[0]
    cols_here = stream.shape[1]
    channels = stream.shape[2]
    tokens_all = rows_here * cols_here * lat_count * lon_count
    tokens = stream.reshape(-1, channels)
    upstream = cotangent.reshape(-1, channels)
    preact = jnp.dot(tokens, w_expand, preferred_element_type=jnp.float32)
    active = gelu_value(preact).astype(jnp.bfloat16)
    through = lax.dot_general(
        upstream, w_reduce, (((1,), (1,)), ((), ())), preferred_element_type=jnp.float32
    )
    dpreact = (through * gelu_slope(preact)).astype(jnp.bfloat16)
    factor = 1.0 / math.sqrt(tokens_all)
    grad_in = (
        lax.dot_general(
            tokens, dpreact, (((0,), (0,)), ((), ())), preferred_element_type=jnp.float32
        )
        * factor
    )
    grad_out = (
        lax.dot_general(
            active, upstream, (((0,), (0,)), ((), ())), preferred_element_type=jnp.float32
        )
        * factor
    )
    grad_expand, grad_reduce = lax.psum((grad_in, grad_out), ("lat", "lon"))
    back_proj = lax.dot_general(
        dpreact, w_expand, (((1,), (1,)), ((), ())), preferred_element_type=jnp.float32
    )
    skip_grad = (
        (upstream.astype(jnp.float32) + back_proj)
        .astype(jnp.bfloat16)
        .reshape(rows_here, cols_here, channels)
    )
    columns = lax.all_to_all(skip_grad, "lon", split_axis=2, concat_axis=1, tiled=True)
    lon_total = columns.shape[1]
    order_count = lon_total // 2
    basis = dft_table(lon_total, order_count)
    fourier = jnp.einsum(
        "anc,knm->kmac", columns, basis, preferred_element_type=jnp.float32
    ).astype(jnp.bfloat16)
    spectrum = lax.all_to_all(
        lax.all_to_all(fourier, "lat", split_axis=1, concat_axis=2, tiled=True),
        "lon",
        split_axis=1,
        concat_axis=3,
        tiled=True,
    )
    by_order = jnp.einsum(
        "kmac,mal->kmlc", spectrum, legendre, preferred_element_type=jnp.float32
    ).astype(jnp.bfloat16)
    by_degree = lax.all_to_all(
        lax.all_to_all(by_order, "lat", split_axis=2, concat_axis=1, tiled=True),
        "lon",
        split_axis=2,
        concat_axis=1,
        tiled=True,
    )
    mixed_coef = jnp.einsum(
        "kmlc,ldc->kmld", by_degree, spectral_mix, preferred_element_type=jnp.float32
    ).astype(jnp.bfloat16)
    returned = lax.all_to_all(
        lax.all_to_all(mixed_coef, "lon", split_axis=1, concat_axis=2, tiled=True),
        "lat",
        split_axis=1,
        concat_axis=2,
        tiled=True,
    )
    summed = jnp.einsum("kmlc,mal->kmac", returned, legendre, preferred_element_type=jnp.float32)
    synthesis = (summed * quadrature[None, None, :, None]).astype(jnp.bfloat16)
    fourier_back = lax.all_to_all(
        lax.all_to_all(synthesis, "lon", split_axis=3, concat_axis=1, tiled=True),
        "lat",
        split_axis=2,
        concat_axis=1,
        tiled=True,
    )
    grid_back = jnp.einsum(
        "kmac,knm->anc", fourier_back, basis, preferred_element_type=jnp.float32
    ).astype(jnp.bfloat16)
    returned_grid = lax.all_to_all(grid_back, "lon", split_axis=1, concat_axis=2, tiled=True)
    grad_input = (skip_grad.astype(jnp.float32) + returned_grid.astype(jnp.float32)).astype(
        jnp.bfloat16
    )
    return (grad_input, grad_expand, grad_reduce)


def solution(mesh):
    placed = (
        P("lat", "lon", None),
        P("lat", "lon", None),
        P(),
        P(),
        P(("lat", "lon"), None, None),
        P(),
        P(("lat", "lon"), None, None),
    )
    return jax.shard_map(
        on_device,
        mesh=mesh,
        in_specs=placed,
        out_specs=(P("lat", "lon", None), P(), P()),
        check_vma=False,
    )
```

profile of v0, /device:TPU:15, one launch (start us, length us, event | category | flops | bytes accessed | tf_op | source)
XLA Modules:
  0.0 1215.4 jit_solution(13901401933875972459)
XLA Ops:
  28.7 9.3 multiply_convert_fusion.3
  38.0 14.6 %all-to-all-done = bf16[16,256,256]{1,0,2:T(8,128)(2,1)} async-done(((bf16[16,256,256]{1,0,2:T(8,128)(2,1)}), bf16[16,256,256]{1,0,2:T(8,128)(2,1)}, u32[]{:S(2)}, u32[]{:S(2)}) %all-to-all-start) | async-done | bytes 2097184 | tf_op jit(solution)/shard_map/all_to_all | solution.py:67
  74.7 7.6 reshape.108
  82.2 61.6 %all_to_all.171 = bf16[8,2,65536]{2,1,0:T(2,128)(2,1)} all-to-all(bf16[8,2,65536]{2,1,0:T(2,128)(2,1)} %reshape.108), channel_id=1, replica_groups=mesh['lat'=8,'lon'=4] {'lat'}, dimensions={0} | all-to-all | bytes 4194304 | tf_op jit(solution)/shard_map/all_to_all | solution.py:75
  161.5 30.5 %all_to_all.172 = bf16[2,64,128,64]{2,3,0,1:T(8,128)(2,1)S(1)} all-to-all(bf16[2,64,128,64]{2,3,0,1:T(8,128)(2,1)} %copy.97), channel_id=1, replica_groups=mesh['lat'=8,'lon'=4] {'lon'}, dimensions={1} | all-to-all | bytes 4194304 | tf_op jit(solution)/shard_map/all_to_all | solution.py:74
  197.8 21.2 %copy.100 = bf16[2,16,512,256]{3,0,1,2:T(2,128)(2,1)} copy(bf16[2,16,512,256]{2,3,0,1:T(8,128)(2,1)} %convert_bitcast_fusion.1) | data formatting | bytes 16777216 | tf_op jit(solution)/shard_map/convert_element_type | solution.py:83
  219.0 187.8 %all_to_all.173 = bf16[2,16,512,256]{3,0,1,2:T(2,128)(2,1)} all-to-all(bf16[2,16,512,256]{3,0,1,2:T(2,128)(2,1)} %copy.100), channel_id=1, replica_groups=mesh['lat'=8,'lon'=4] {'lat'}, dimensions={2} | all-to-all | bytes 16777216 | tf_op jit(solution)/shard_map/all_to_all | solution.py:85
  406.8 11.4 copy.101
  418.2 8.3 copy.102
  426.5 11.4 copy.103
  437.9 101.8 %all_to_all.174 = bf16[2,128,64,256]{3,1,0,2:T(8,128)(2,1)} all-to-all(bf16[2,128,64,256]{3,1,0,2:T(8,128)(2,1)} %copy.103), channel_id=1, replica_groups=mesh['lat'=8,'lon'=4] {'lon'}, dimensions={2} | all-to-all | bytes 16777216 | tf_op jit(solution)/shard_map/all_to_all | solution.py:84
  539.6 7.9 copy.105
  547.5 9.0 convert_bitcast_fusion
  556.6 14.5 %copy.106 = bf16[2,512,16,256]{3,0,2,1:T(2,128)(2,1)S(1)} copy(bf16[2,512,16,256]{3,1,0,2:T(8,128)(2,1)} %convert_bitcast_fusion) | data formatting | bytes 16777216 | tf_op jit(solution)/shard_map/convert_element_type | solution.py:93
  571.1 96.9 %all_to_all.175 = bf16[2,512,16,256]{3,0,2,1:T(2,128)(2,1)} all-to-all(bf16[2,512,16,256]{3,0,2,1:T(2,128)(2,1)S(1)} %copy.106), channel_id=1, replica_groups=mesh['lat'=8,'lon'=4] {'lon'}, dimensions={1} | all-to-all | bytes 16777216 | tf_op jit(solution)/shard_map/all_to_all | solution.py:95
  668.0 8.0 copy.107
  676.0 7.9 copy.108
  683.9 8.3 copy.109
  692.2 188.1 %all_to_all.176 = bf16[2,128,64,256]{3,2,0,1:T(8,128)(2,1)} all-to-all(bf16[2,128,64,256]{3,2,0,1:T(8,128)(2,1)} %copy.109), channel_id=1, replica_groups=mesh['lat'=8,'lon'=4] {'lat'}, dimensions={1} | all-to-all | bytes 16777216 | tf_op jit(solution)/shard_map/all_to_all | solution.py:94
  880.3 8.3 copy.111
  896.7 29.2 %all_to_all.177 = bf16[2,16,128,256]{2,0,1,3:T(2,128)(2,1)S(1)} all-to-all(bf16[2,16,128,256]{2,0,1,3:T(2,128)(2,1)S(1)} %copy.113), channel_id=1, replica_groups=mesh['lat'=8,'lon'=4] {'lon'}, dimensions={3} | all-to-all | bytes 4194304 | tf_op jit(solution)/shard_map/all_to_all | solution.py:104
  935.6 7.6 reshape.110
  943.2 51.7 %all_to_all.178 = bf16[8,2,65536]{2,1,0:T(2,128)(2,1)} all-to-all(bf16[8,2,65536]{2,1,0:T(2,128)(2,1)} %reshape.110), channel_id=1, replica_groups=mesh['lat'=8,'lon'=4] {'lat'}, dimensions={0} | all-to-all | bytes 4194304 | tf_op jit(solution)/shard_map/all_to_all | solution.py:103
  1055.7 124.2 %all-reduce.3.cloned.1.call-done = (f32[256,512]{0,1:T(8,128)}, f32[512,256]{1,0:T(8,128)}) async-done(((f32[256,512]{0,1:T(8,128)}, f32[512,256]{1,0:T(8,128)}), (f32[256,512]{0,1:T(8,128)}, f32[512,256]{1,0:T(8,128)})) %all-reduce.3.cloned.1.call-update) | async-done | bytes 1048592 | tf_op jit(solution)/shard_map/psum | solution.py:58
  (62 shorter events, 174.0 us)
Async XLA Ops:
  7.2 185.0 %copy-start = (bf16[16,128,512]{2,1,0:T(8,128)(2,1)S(1)}, bf16[16,128,512]{2,1,0:T(8,128)(2,1)}, u32[]{:S(2)}) copy-start(bf16[16,128,512]{2,1,0:T(8,128)(2,1)} %param.11) | copy-start | bytes 6291460
  7.2 3.0 copy-start.4
  7.2 3.0 copy-start.9
  10.2 6.0 copy-start.1
  10.2 5.9 copy-start.7
  16.2 2.7 copy-start.2
  23.5 29.2 %all-to-all-start = ((bf16[16,256,256]{1,0,2:T(8,128)(2,1)}), bf16[16,256,256]{1,0,2:T(8,128)(2,1)}, u32[]{:S(2)}, u32[]{:S(2)}) async-start(bf16[16,256,256]{1,0,2:T(8,128)(2,1)} %copy.92), calls=%async_computation | async-start | bytes 4194304 | tf_op jit(solution)/shard_map/all_to_all | solution.py:67
  539.6 7.9 copy-start.6
  880.3 8.3 copy-start.10
  1033.2 148.6 %all-to-all-start.9 = ((bf16[4,2,131072]{2,1,0:T(2,128)(2,1)}), bf16[4,2,131072]{2,1,0:T(2,128)(2,1)}, u32[]{:S(2)}, u32[]{:S(2)}) async-start(bf16[4,2,131072]{2,1,0:T(2,128)(2,1)} %reshape.112), calls=%async_computation.9 | async-start | bytes 4194304 | tf_op jit(solution)/shard_map/all_to_all | solution.py:113
  1040.6 139.3 %all-reduce.3.cloned.1.call-start = ((), (), s32[]{:S(2)}) async-start(), calls=%async_computation.10 | async-start | bytes 2097152 | tf_op jit(solution)/shard_map/psum | solution.py:58
  1040.6 5.1 copy-start.5
  1198.2 3.1 copy-start.3
  1203.6 4.0 copy-start.8
Sparse Core Ops, SparseCore 0:
  1051.9 127.9 all-reduce.2
where the time goes:
time: 1230 us; the launch traced here: 1220 us
  blocking collectives  747 us (61%)
  local copies, waits for them, and re-layouts  236 us (19%)
  waiting for transfers between devices  139 us (11%)
  matrix products  54.4 us (4%)
  between operations  14.4 us (1%)
  starting transfers between devices  12.6 us (1%)
    all_to_all x1, blocking collectives, on_device(): lax.all_to_all(lax.all_to_all(mixed_coef, 'lon', split_axis=1, concat_axi...  188 us
    all_to_all x1, blocking collectives, on_device(): lax.all_to_all(by_order, 'lat', split_axis=2, concat_axis=1, tiled=True)  188 us
    psum x1, waiting for transfers between devices, on_device(): grad_expand, grad_reduce = lax.psum((grad_in, grad_out), ('lat', 'lon'))  124 us
    all_to_all x1, blocking collectives, on_device(): lax.all_to_all(lax.all_to_all(by_order, 'lat', split_axis=2, concat_axis=...  102 us
    all_to_all x1, blocking collectives, on_device(): lax.all_to_all(mixed_coef, 'lon', split_axis=1, concat_axis=2, tiled=True)  96.9 us
    all_to_all x1, blocking collectives, on_device(): lax.all_to_all(fourier, 'lat', split_axis=1, concat_axis=2, tiled=True)  61.6 us
    all_to_all x1, blocking collectives, on_device(): lax.all_to_all(lax.all_to_all(synthesis, 'lon', split_axis=3, concat_axis...  51.7 us
    unnamed x31, local copies, waits for them, and re-layouts  48.7 us
  transfers between devices with their start and end apart: 3, of which 2 were waited for; matrix products, arithmetic and copies ran while one was open for 2% of the time, Pallas kernels for 0%

commit v1 on v0

--- a/solution.py
+++ b/solution.py
@@ -1,8 +1,11 @@
+import functools
 import math
 
 import jax
 import jax.numpy as jnp
 from jax import lax
+from jax.experimental import pallas as pl
+from jax.experimental.pallas import tpu as pltpu
 from jax.sharding import PartitionSpec as P
 
 
@@ -117,6 +120,347 @@
     return (grad_input, grad_expand, grad_reduce)
 
 
+MESH = pl.DeviceIdType.MESH
+
+
+def greet(count, me, device_of):
+    barrier = pltpu.get_barrier_semaphore()
+
+    def hello(off, carry):
+        pl.semaphore_signal(
+            barrier, inc=1, device_id=device_of(lax.rem(me + off, count)), device_id_type=MESH
+        )
+        return carry
+
+    lax.fori_loop(1, count, hello, 0)
+    pl.semaphore_wait(barrier, count - 1)
+
+
+def place_of(lon_only):
+    lat_index = lax.axis_index("lat")
+    lon_index = lax.axis_index("lon")
+    lon_count = lax.axis_size("lon")
+    if lon_only:
+        return lon_index, lon_count, lambda j: (lat_index, j)
+    count = lax.axis_size("lat") * lon_count
+    return (
+        lat_index * lon_count + lon_index,
+        count,
+        lambda j: (lax.div(j, lon_count), lax.rem(j, lon_count)),
+    )
+
+
+def exchange_body(lon_only, views, *refs):
+    width = len(views)
+    ins, outs = refs[:width], refs[width : 2 * width]
+    send_sem, recv_sem, own_sem = refs[2 * width :]
+    me, count, device_of = place_of(lon_only)
+    greet(count, me, device_of)
+
+    def remote(n, off, target, landing):
+        return pltpu.make_async_remote_copy(
+            src_ref=views[n][0](ins[n], target),
+            dst_ref=views[n][1](outs[n], landing),
+            send_sem=send_sem.at[n, off],
+            recv_sem=recv_sem.at[n, off],
+            device_id=device_of(target),
+            device_id_type=MESH,
+        )
+
+    def launch(off, carry):
+        for n in range(width):
+            remote(n, off, lax.rem(me + off, count), me).start()
+        return carry
+
+    lax.fori_loop(1, count, launch, 0)
+    own = [
+        pltpu.make_async_copy(views[n][0](ins[n], me), views[n][1](outs[n], me), own_sem.at[n])
+        for n in range(width)
+    ]
+    for copy in own:
+        copy.start()
+    for copy in own:
+        copy.wait()
+
+    def finish(off, carry):
+        for n in range(width):
+            copy = remote(n, off, lax.rem(me + off, count), lax.rem(me + count - off, count))
+            copy.wait_send()
+            copy.wait_recv()
+        return carry
+
+    lax.fori_loop(1, count, finish, 0)
+
+
+def exchange(arrays, shapes, views, lon_only, collective_id):
+    count = lax.axis_size("lon") * (1 if lon_only else lax.axis_size("lat"))
+    width = len(arrays)
+    return pl.pallas_call(
+        functools.partial(exchange_body, lon_only, views),
+        out_shape=[jax.ShapeDtypeStruct(s, a.dtype) for s, a in zip(shapes, arrays)],
+        in_specs=[pl.BlockSpec(memory_space=pl.ANY)] * width,
+        out_specs=[pl.BlockSpec(memory_space=pl.ANY)] * width,
+        scratch_shapes=[
+            pltpu.SemaphoreType.DMA((width, count)),
+            pltpu.SemaphoreType.DMA((width, count)),
+            pltpu.SemaphoreType.DMA((width,)),
+        ],
+        compiler_params=pltpu.CompilerParams(collective_id=collective_id, has_side_effects=True),
+    )(*arrays)
+
+
+CUTS = 2
+
+
+def mix_body(
+    b_ref, mix_ref, g_ref, w_ref, gall_ref, got, made,
+    fs_sem, fr_sem, bs_sem, br_sem, gs_sem, gr_sem, own_sem,
+):
+    me, count, device_of = place_of(False)
+    depth = got.shape[1]
+    part = depth // CUTS
+    orders, channels = got.shape[3], got.shape[4]
+    greet(count, me, device_of)
+
+    def forward(k, h, off, target, landing):
+        return pltpu.make_async_remote_copy(
+            src_ref=b_ref.at[k, target, pl.ds(h * part, part)],
+            dst_ref=got.at[k, pl.ds(h * part, part), landing],
+            send_sem=fs_sem.at[k * CUTS + h, off],
+            recv_sem=fr_sem.at[k * CUTS + h, off],
+            device_id=device_of(target),
+            device_id_type=MESH,
+        )
+
+    def back(k, h, off, target, landing):
+        return pltpu.make_async_remote_copy(
+            src_ref=made.at[k, pl.ds(h * part, part), target],
+            dst_ref=w_ref.at[k, landing, pl.ds(h * part, part)],
+            send_sem=bs_sem.at[k * CUTS + h, off],
+            recv_sem=br_sem.at[k * CUTS + h, off],
+            device_id=device_of(target),
+            device_id_type=MESH,
+        )
+
+    def gather(off, landing):
+        return pltpu.make_async_remote_copy(
+            src_ref=g_ref,
+            dst_ref=gall_ref.at[landing],
+            send_sem=gs_sem.at[off],
+            recv_sem=gr_sem.at[off],
+            device_id=device_of(lax.rem(me + off, count)),
+            device_id_type=MESH,
+        )
+
+    def over(first, last, step):
+        def run(at, carry):
+            step(at)
+            return carry
+
+        lax.fori_loop(first, last, run, 0)
+
+    chunks = [(k, h) for k in range(2) for h in range(CUTS)]
+    for k, h in chunks:
+        over(1, count - me, lambda off: forward(k, h, off, me + off, me).start())
+    over(1, count, lambda off: gather(off, me).start())
+    own = [
+        pltpu.make_async_copy(b_ref.at[k, me], got.at[k, :, me], own_sem.at[k]) for k in range(2)
+    ] + [pltpu.make_async_copy(g_ref, gall_ref.at[me], own_sem.at[2])]
+    for copy in own:
+        copy.start()
+    for copy in own:
+        copy.wait()
+    for k, h in chunks:
+        over(1, me + 1, lambda off: forward(k, h, off, me, me - off).wait_recv())
+
+        def mix(l):
+            rows = got[k, l].reshape(count * orders, channels)
+            made[k, l] = (
+                lax.dot_general(
+                    rows, mix_ref[l], (((1,), (1,)), ((), ())), preferred_element_type=jnp.float32
+                )
+                .astype(jnp.bfloat16)
+                .reshape(count, orders, channels)
+            )
+
+        over(h * part, (h + 1) * part, mix)
+        over(1, me + 1, lambda off: back(k, h, off, me - off, me).start())
+    own = [
+        pltpu.make_async_copy(made.at[k, :, me], w_ref.at[k, me], own_sem.at[k]) for k in range(2)
+    ]
+    for copy in own:
+        copy.start()
+    for copy in own:
+        copy.wait()
+    for k, h in chunks:
+        over(1, count - me, lambda off: forward(k, h, off, me + off, me).wait_send())
+        over(1, me + 1, lambda off: back(k, h, off, me - off, me).wait_send())
+        over(1, count - me, lambda off: back(k, h, off, me, me + off).wait_recv())
+
+    def gathered(off):
+        copy = gather(off, lax.rem(me + count - off, count))
+        copy.wait_send()
+        copy.wait_recv()
+
+    over(1, count, gathered)
+
+
+def mix_exchange(by_order, spectral_mix, reduced, collective_id):
+    _, count, depth, orders, channels = by_order.shape
+    sems = pltpu.SemaphoreType.DMA((2 * CUTS, count))
+    return pl.pallas_call(
+        mix_body,
+        out_shape=[
+            jax.ShapeDtypeStruct(by_order.shape, jnp.bfloat16),
+            jax.ShapeDtypeStruct((count,) + reduced.shape, reduced.dtype),
+        ],
+        in_specs=[
+            pl.BlockSpec(memory_space=pl.ANY),
+            pl.BlockSpec(memory_space=pltpu.VMEM),
+            pl.BlockSpec(memory_space=pl.ANY),
+        ],
+        out_specs=[pl.BlockSpec(memory_space=pl.ANY)] * 2,
+        scratch_shapes=[
+            pltpu.VMEM((2, depth, count, orders, channels), jnp.bfloat16),
+            pltpu.VMEM((2, depth, count, orders, channels), jnp.bfloat16),
+            sems,
+            sems,
+            sems,
+            sems,
+            pltpu.SemaphoreType.DMA((count,)),
+            pltpu.SemaphoreType.DMA((count,)),
+            pltpu.SemaphoreType.DMA((3,)),
+        ],
+        compiler_params=pltpu.CompilerParams(
+            collective_id=collective_id, has_side_effects=True, vmem_limit_bytes=40 * 2**20
+        ),
+    )(by_order, spectral_mix, reduced)
+
+
+def direct(stream, cotangent, w_expand, w_reduce, legendre, quadrature, spectral_mix):
+    lat_count = lax.axis_size("lat")
+    lon_count = lax.axis_size("lon")
+    count = lat_count * lon_count
+    me = lax.axis_index("lat") * lon_count + lax.axis_index("lon")
+    rows_here, cols_here, channels = stream.shape
+    hidden = w_expand.shape[1]
+    lon_total = cols_here * lon_count
+    rows_own = rows_here // lon_count
+    orders, rows_all, degrees = legendre.shape
+    depth = degrees // count
+    tokens = stream.reshape(-1, channels)
+    upstream = cotangent.reshape(-1, channels)
+    preact = jnp.dot(tokens, w_expand, preferred_element_type=jnp.float32)
+    active = gelu_value(preact).astype(jnp.bfloat16)
+    through = lax.dot_general(
+        upstream, w_reduce, (((1,), (1,)), ((), ())), preferred_element_type=jnp.float32
+    )
+    dpreact = (through * gelu_slope(preact)).astype(jnp.bfloat16)
+    back_proj = lax.dot_general(
+        dpreact, w_expand, (((1,), (1,)), ((), ())), preferred_element_type=jnp.float32
+    )
+    skip_grad = (
+        (upstream.astype(jnp.float32) + back_proj)
+        .astype(jnp.bfloat16)
+        .reshape(rows_here, cols_here, channels)
+    )
+    grad_in = lax.dot_general(
+        tokens, dpreact, (((0,), (0,)), ((), ())), preferred_element_type=jnp.float32
+    )
+    grad_out = lax.dot_general(
+        upstream, active, (((0,), (0,)), ((), ())), preferred_element_type=jnp.float32
+    )
+    grads = jnp.concatenate(
+        [grad_in.reshape(count, -1, hidden), grad_out.reshape(count, -1, hidden)], axis=1
+    )
+
+    (rows,) = exchange(
+        [skip_grad],
+        [(rows_own, lon_total, channels)],
+        [
+            (
+                lambda ref, j: ref.at[pl.ds(j * rows_own, rows_own)],
+                lambda ref, j: ref.at[:, pl.ds(j * cols_here, cols_here)],
+            )
+        ],
+        True,
+        0,
+    )
+    basis = dft_table(lon_total, lon_total // 2)
+    fourier = lax.dot_general(
+        jnp.transpose(basis, (2, 0, 1)).reshape(lon_total, lon_total),
+        rows,
+        (((1,), (1,)), ((), ())),
+        preferred_element_type=jnp.float32,
+    ).astype(jnp.bfloat16)
+    lead = lambda ref, j: ref.at[j]
+    blocks, terms = exchange(
+        [fourier.reshape(count, 2 * orders, rows_own * channels), grads],
+        [(count, 2 * orders, rows_own * channels), grads.shape],
+        [(lead, lead), (lead, lead)],
+        False,
+        1,
+    )
+    reduced = jnp.sum(terms, axis=0) * (1.0 / math.sqrt(rows_here * cols_here * count))
+    spectrum = jnp.transpose(
+        blocks.reshape(count, orders, 2, rows_own, channels), (2, 1, 0, 3, 4)
+    ).reshape(2, orders, rows_all, channels)
+    by_order = (
+        jnp.einsum("mal,kmac->klmc", legendre, spectrum, preferred_element_type=jnp.float32)
+        .astype(jnp.bfloat16)
+        .reshape(2, count, depth, orders, channels)
+    )
+    mixed, gathered = mix_exchange(by_order, spectral_mix, reduced, 2)
+    arrived = lax.broadcasted_iota(jnp.int32, mixed.shape, 1) >= me
+    mixed = jnp.where(arrived, mixed, jnp.zeros_like(mixed)).reshape(2, degrees, orders, channels)
+    summed = jnp.einsum("klmc,mal->mkac", mixed, legendre, preferred_element_type=jnp.float32)
+    synthesis = (summed * quadrature[None, None, :, None]).astype(jnp.bfloat16)
+    synthesis = jnp.transpose(
+        synthesis.reshape(2 * orders, count, rows_own, channels), (1, 0, 2, 3)
+    ).reshape(count, 2 * orders, rows_own * channels)
+    (waves,) = exchange([synthesis], [synthesis.shape], [(lead, lead)], False, 3)
+    waves = waves.reshape(lon_total, rows_own, channels)
+    grid_back = lax.dot_general(
+        waves,
+        jnp.transpose(basis, (2, 0, 1)).reshape(lon_total, lon_total),
+        (((0,), (0,)), ((), ())),
+        preferred_element_type=jnp.float32,
+    ).astype(jnp.bfloat16)
+    grid_back = jnp.transpose(grid_back, (0, 2, 1))
+    (returned_grid,) = exchange(
+        [grid_back],
+        [stream.shape],
+        [
+            (
+                lambda ref, j: ref.at[:, pl.ds(j * cols_here, cols_here)],
+                lambda ref, j: ref.at[pl.ds(j * rows_own, rows_own)],
+            )
+        ],
+        True,
+        4,
+    )
+    grad_input = (skip_grad.astype(jnp.float32) + returned_grid.astype(jnp.float32)).astype(
+        jnp.bfloat16
+    )
+    half = gathered.shape[1] // 2
+    grad_expand = gathered[:, :half].reshape(channels, hidden)
+    grad_reduce = gathered[:, half:].reshape(channels, hidden).T
+    return (grad_input, grad_expand, grad_reduce)
+
+
+def on_either(stream, cotangent, w_expand, w_reduce, legendre, quadrature, spectral_mix):
+    count = lax.axis_size("lat") * lax.axis_size("lon")
+    whole_tiles = (
+        legendre.shape[0] % 16 == 0
+        and spectral_mix.shape[0] % CUTS == 0
+        and stream.shape[0] % lax.axis_size("lon") == 0
+        and stream.shape[1] % 16 == 0
+        and w_expand.shape[0] % (8 * count) == 0
+    )
+    chosen = direct if whole_tiles else on_device
+    return chosen(stream, cotangent, w_expand, w_reduce, legendre, quadrature, spectral_mix)
+
+
 def solution(mesh):
     placed = (
         P("lat", "lon", None),
@@ -128,7 +472,7 @@
         P(("lat", "lon"), None, None),
     )
     return jax.shard_map(
-        on_device,
+        on_either,
         mesh=mesh,
         in_specs=placed,
         out_specs=(P("lat", "lon", None), P(), P()),

time: 1230 us -> 600 us (0.49); the launches traced: 1220 us -> 598 us
  blocking collectives: 747 us -> 0 us
  Pallas kernels: 0 us -> 463 us
  local copies, waits for them, and re-layouts: 236 us -> 64.2 us
  waiting for transfers between devices: 139 us -> 0 us
  between operations: 14.4 us -> 0.86 us
  starting transfers between devices: 12.6 us -> 0 us
    all_to_all x8 -> x0, blocking collectives: 747 us -> none  [the longest x1 188 us: on_device(): lax.all_to_all(lax.all_to_all(mixed_coef, 'lon', split_axis=1, concat_axi...]
    pallas_call x0 -> x5, Pallas kernels: none -> 463 us  [the longest x1 238 us: mix_exchange(): pl.pallas_call(mix_body, out_shape=[jax.ShapeDtypeStruct(by_order.shape,...]
    psum x1 -> x0, waiting for transfers between devices: 124 us -> none  [on_device(): grad_expand, grad_reduce = lax.psum((grad_in, grad_out), ('lat', 'lon'))]
    all_to_all x19 -> x0, local copies, waits for them, and re-layouts: 119 us -> none  [the longest x3 31.1 us: on_device(): lax.all_to_all(by_order, 'lat', split_axis=2, concat_axis=1, tiled=True)]
    unnamed x31 -> x22, local copies, waits for them, and re-layouts: 48.7 us -> 4.86 us
    convert_element_type x7 -> x2, local copies, waits for them, and re-layouts: 59.6 us -> 17.9 us  [the longest x1 15 us: direct(): by_order = jnp.einsum('mal,kmac->klmc', legendre, spectrum, preferred_ele...]
    reshape x2 -> x10, local copies, waits for them, and re-layouts: 8.51 us -> 35.2 us  [the longest x2 7.97 us: direct(): synthesis.reshape(2 * orders, count, rows_own, channels)]
    all_to_all x2 -> x0, waiting for transfers between devices: 14.6 us -> none  [the longest x1 14.6 us: on_device(): lax.all_to_all(skip_grad, 'lon', split_axis=2, concat_axis=1, tiled=True)]
  transfers between devices with their start and end apart: 3 -> 0, of which waited for: 2 -> 0; matrix products, arithmetic and copies ran while one was open for 2% -> 0% of each run, Pallas kernels for 0% -> 0%
where the time goes in v1:
time: 600 us; the launch traced here: 598 us
  Pallas kernels  463 us (77%)
  local copies, waits for them, and re-layouts  64.2 us (11%)
  matrix products  47.5 us (8%)
  other arithmetic  22.8 us (4%)
    pallas_call x1, Pallas kernels, mix_exchange(): pl.pallas_call(mix_body, out_shape=[jax.ShapeDtypeStruct(by_order.shape,...  238 us
    pallas_call x4, Pallas kernels, exchange(): pl.pallas_call(functools.partial(exchange_body, lon_only, views), out_sha...  225 us
    convert_element_type x1, local copies, waits for them, and re-layouts, direct(): by_order = jnp.einsum('mal,kmac->klmc', legendre, spectrum, preferred_ele...  15 us

profile of v1, /device:TPU:15, one launch (start us, length us, event | category | flops | bytes accessed | tf_op | source)
XLA Modules:
  0.0 598.3 jit_solution(11636290266531504892)
XLA Ops:
  3.7 5.9 fusion.6
  12.3 25.9 %shard_map.94 = bf16[4,1024,256]{2,1,0:T(8,128)(2,1)} custom-call(bf16[16,256,256]{2,1,0:T(8,128)(2,1)} %bitcast.56), custom_call_target="tpu_custom_call" | custom-call | tf_op jit(solution)/shard_map/pallas_call | solution.py:198
  38.2 8.6 %multiply_convert_fusion.3 = (bf16[1,1024,512]{2,1,0:T(8,128)(2,1)S(1)}, bf16[1,1024,512]{2,1,0:T(8,128)(2,1)S(1)}) fusion(), kind=kLoop, calls=%fused_computation.34 | loop fusion | flops 9961472 | bytes 2097152 | tf_op jit(solution)/shard_map/convert.1
  48.3 6.2 %copy.36 = bf16[512,2,1024]{2,1,0:T(2,128)(2,1)} copy(bf16[512,2,1024]{0,2,1:T(8,128)(2,1)} %maximum_bitcast_fusion) | data formatting | bytes 4194304 | tf_op jit(solution)/shard_map/transpose | solution.py:391
  54.6 4.1 reshape.149
  58.7 4.5 convolution_convert_fusion
  66.1 4.5 reshape.137.refs_0_
  70.6 4.3 convolution_bitcast_fusion
  74.9 5.9 fusion.29
  81.9 81.6 %shard_map.95 = (bf16[32,32,1024]{2,1,0:T(8,128)(2,1)}, f32[32,16,512]{2,1,0:T(8,128)}) custom-call(bf16[32,32,1024]{2,1,0:T(8,128)(2,1)} %reshape.137.refs_0_, f32[32,16,512]{2,1,0:T(8,128)} %pad_maximum_fusion.refs_1_), custom_call_target="tpu_custom_call" | custom-call | tf_op jit(solution)/shard_map/pallas_call | solution.py:198
  163.5 4.5 reshape.140
  170.2 5.6 convert_bitcast_fusion
  175.8 15.0 %copy.40 = bf16[2,512,16,256]{3,2,1,0:T(8,128)(2,1)} copy(bf16[2,512,16,256]{1,3,0,2:T(8,128)(2,1)} %convert_bitcast_fusion) | data formatting | bytes 16777216 | tf_op jit(solution)/shard_map/convert_element_type | solution.py:410
  192.5 238.5 %shard_map.96 = (bf16[2,32,16,16,256]{4,3,2,1,0:T(8,128)(2,1)S(1)}, f32[32,16,512]{2,1,0:T(8,128)S(1)}) custom-call(bf16[2,32,16,16,256]{4,3,2,1,0:T(8,128)(2,1)} %bitcast.55, bf16[16,256,256]{2,1,0:T(8,128)(2,1)S(1)} %copy-done.2, f32[16,512]{1,0:T(8,128)S(1)} %broadcast_multiply_fusion.g_ref), custom_call_target="tpu_custom_call" | custom-call | tf_op jit(solution)/shard_map/pallas_call | solution.py:311
  434.2 7.3 %broadcast_select_fusion = bf16[2,32,16,16,256]{4,3,2,1,0:T(8,128)(2,1)} fusion(bf16[2,32,16,16,256]{4,3,2,1,0:T(8,128)(2,1)} %copy-done.1, pred[32]{0:T(512)(128)(4,1)S(1)} %iota_compare_fusion), kind=kLoop, calls=%fused_computation.13 | loop fusion | flops 4194304 | bytes 16777248 | tf_op jit(solution)/shard_map/jit(_where)/select_n | solution.py:415
  441.6 9.6 %fusion.14 = bf16[16,2,128,256]{3,2,1,0:T(8,128)(2,1)} fusion(f32[128]{0:T(128)S(1)} %copy-done.10, bf16[2,512,16,256]{3,2,1,0:T(8,128)(2,1)} %bitcast.58, bf16[16,128,512]{2,1,0:T(8,128)(2,1)S(1)} %copy-done), kind=kOutput, calls=%fused_computation.25 | convolution fusion | flops 1075838976 | bytes 12583424 | tf_op jit(solution)/shard_map/klmc,mal->mkac/dot_general | solution.py:416
  451.1 4.0 reshape.144
  455.1 4.0 copy.59
  459.1 4.4 reshape.145.refs_0_
  463.5 91.7 %shard_map.97 = bf16[32,32,1024]{2,1,0:T(8,128)(2,1)} custom-call(bf16[32,32,1024]{2,1,0:T(8,128)(2,1)} %reshape.145.refs_0_), custom_call_target="tpu_custom_call" | custom-call | tf_op jit(solution)/shard_map/pallas_call | solution.py:198
  555.3 4.5 reshape.146
  559.8 5.9 convert_bitcast_fusion.1.refs_0_
  565.7 25.3 %shard_map.98 = bf16[16,256,256]{2,1,0:T(8,128)(2,1)} custom-call(bf16[4,1024,256]{2,1,0:T(8,128)(2,1)} %convert_bitcast_fusion.1.refs_0_), custom_call_target="tpu_custom_call" | custom-call | tf_op jit(solution)/shard_map/pallas_call | solution.py:198
  591.0 4.2 add_convert_fusion
  (33 shorter events, 21.3 us)
Async XLA Ops:
  0.6 169.5 %copy-start = (bf16[16,128,512]{2,1,0:T(8,128)(2,1)S(1)}, bf16[16,128,512]{2,1,0:T(8,128)(2,1)}, u32[]{:S(2)}) copy-start(bf16[16,128,512]{2,1,0:T(8,128)(2,1)} %param.11) | copy-start | bytes 6291460
  0.6 3.0 copy-start.5
  0.7 3.0 copy-start.9
  3.7 6.0 copy-start.3
  3.7 5.9 copy-start.7
  9.6 2.7 copy-start.4
  70.6 4.3 copy-start.6
  175.8 15.0 %copy-start.8 = (f32[32,16,512]{2,1,0:T(8,128)S(1)}, f32[32,16,512]{2,1,0:T(8,128)}, u32[]{:S(2)}) copy-start(f32[32,16,512]{2,1,0:T(8,128)} %get-tuple-element.8) | copy-start | bytes 3145732
  190.9 1.6 copy-start.2
  431.0 3.2 copy-start.1
  434.2 7.4 %copy-start.10 = (f32[128]{0:T(128)S(1)}, f32[128]{0:T(128)}, u32[]{:S(2)}) copy-start(f32[128]{0:T(128)} %param.12) | copy-start | bytes 1540

commit v2 on v1

--- a/solution.py
+++ b/solution.py
@@ -3,6 +3,7 @@
 
 import jax
 import jax.numpy as jnp
+import numpy as np
 from jax import lax
 from jax.experimental import pallas as pl
 from jax.experimental.pallas import tpu as pltpu
@@ -214,7 +215,7 @@
 
 def mix_body(
     b_ref, mix_ref, g_ref, w_ref, gall_ref, got, made,
-    fs_sem, fr_sem, bs_sem, br_sem, gs_sem, gr_sem, own_sem,
+    fs_sem, fr_sem, bs_sem, br_sem, gs_sem, gr_sem, own_sem, blank, blank_sem,
 ):
     me, count, device_of = place_of(False)
     depth = got.shape[1]
@@ -263,6 +264,11 @@
     for k, h in chunks:
         over(1, count - me, lambda off: forward(k, h, off, me + off, me).start())
     over(1, count, lambda off: gather(off, me).start())
+    blank[...] = jnp.zeros_like(blank)
+
+    def clear(k, j):
+        return pltpu.make_async_copy(blank, w_ref.at[k, j], blank_sem.at[k, j])
+
     own = [
         pltpu.make_async_copy(b_ref.at[k, me], got.at[k, :, me], own_sem.at[k]) for k in range(2)
     ] + [pltpu.make_async_copy(g_ref, gall_ref.at[me], own_sem.at[2])]
@@ -270,6 +276,8 @@
         copy.start()
     for copy in own:
         copy.wait()
+    for k in range(2):
+        over(0, me, lambda j: clear(k, j).start())
     for k, h in chunks:
         over(1, me + 1, lambda off: forward(k, h, off, me, me - off).wait_recv())
 
@@ -303,6 +311,8 @@
         copy.wait_recv()
 
     over(1, count, gathered)
+    for k in range(2):
+        over(0, me, lambda j: clear(k, j).wait())
 
 
 def mix_exchange(by_order, spectral_mix, reduced, collective_id):
@@ -330,6 +340,8 @@
             pltpu.SemaphoreType.DMA((count,)),
             pltpu.SemaphoreType.DMA((count,)),
             pltpu.SemaphoreType.DMA((3,)),
+            pltpu.VMEM((depth, orders, channels), jnp.bfloat16),
+            pltpu.SemaphoreType.DMA((2, count)),
         ],
         compiler_params=pltpu.CompilerParams(
             collective_id=collective_id, has_side_effects=True, vmem_limit_bytes=40 * 2**20
@@ -337,11 +349,21 @@
     )(by_order, spectral_mix, reduced)
 
 
+def wave_rows(count):
+    order_index = np.arange(count // 2, dtype=np.int64)[:, None]
+    lon_index = np.arange(count, dtype=np.int64)[None, :]
+    angles = (order_index * lon_index % count).astype(np.float32) * np.float32(
+        2.0 * math.pi / count
+    )
+    factor = np.float32(1.0 / math.sqrt(count))
+    table = np.stack([np.cos(angles) * factor, -np.sin(angles) * factor], axis=1)
+    return table.reshape(count, count).astype(jnp.bfloat16)
+
+
 def direct(stream, cotangent, w_expand, w_reduce, legendre, quadrature, spectral_mix):
     lat_count = lax.axis_size("lat")
     lon_count = lax.axis_size("lon")
     count = lat_count * lon_count
-    me = lax.axis_index("lat") * lon_count + lax.axis_index("lon")
     rows_here, cols_here, channels = stream.shape
     hidden = w_expand.shape[1]
     lon_total = cols_here * lon_count
@@ -386,47 +408,44 @@
         True,
         0,
     )
-    basis = dft_table(lon_total, lon_total // 2)
-    fourier = lax.dot_general(
-        jnp.transpose(basis, (2, 0, 1)).reshape(lon_total, lon_total),
-        rows,
-        (((1,), (1,)), ((), ())),
-        preferred_element_type=jnp.float32,
+    waves_of = jnp.asarray(wave_rows(lon_total))
+    fourier = jnp.einsum(
+        "pn,anc->apc", waves_of, rows, preferred_element_type=jnp.float32
     ).astype(jnp.bfloat16)
     lead = lambda ref, j: ref.at[j]
+    by_orders = lambda ref, j: ref.at[:, pl.ds(j * 2 * orders, 2 * orders)]
+    by_rows = lambda ref, j: ref.at[pl.ds(j * rows_own, rows_own)]
     blocks, terms = exchange(
-        [fourier.reshape(count, 2 * orders, rows_own * channels), grads],
-        [(count, 2 * orders, rows_own * channels), grads.shape],
-        [(lead, lead), (lead, lead)],
+        [fourier, grads.astype(jnp.bfloat16)],
+        [(rows_all, 2 * orders, channels), grads.shape],
+        [(by_orders, by_rows), (lead, lead)],
         False,
         1,
     )
-    reduced = jnp.sum(terms, axis=0) * (1.0 / math.sqrt(rows_here * cols_here * count))
-    spectrum = jnp.transpose(
-        blocks.reshape(count, orders, 2, rows_own, channels), (2, 1, 0, 3, 4)
-    ).reshape(2, orders, rows_all, channels)
+    reduced = (
+        jnp.sum(terms.astype(jnp.float32), axis=0)
+        * (1.0 / math.sqrt(rows_here * cols_here * count))
+    ).astype(jnp.bfloat16)
+    spectrum = blocks.reshape(rows_all, orders, 2, channels)
     by_order = (
-        jnp.einsum("mal,kmac->klmc", legendre, spectrum, preferred_element_type=jnp.float32)
+        jnp.einsum("mal,amkc->klmc", legendre, spectrum, preferred_element_type=jnp.float32)
         .astype(jnp.bfloat16)
         .reshape(2, count, depth, orders, channels)
     )
     mixed, gathered = mix_exchange(by_order, spectral_mix, reduced, 2)
-    arrived = lax.broadcasted_iota(jnp.int32, mixed.shape, 1) >= me
-    mixed = jnp.where(arrived, mixed, jnp.zeros_like(mixed)).reshape(2, degrees, orders, channels)
-    summed = jnp.einsum("klmc,mal->mkac", mixed, legendre, preferred_element_type=jnp.float32)
-    synthesis = (summed * quadrature[None, None, :, None]).astype(jnp.bfloat16)
-    synthesis = jnp.transpose(
-        synthesis.reshape(2 * orders, count, rows_own, channels), (1, 0, 2, 3)
-    ).reshape(count, 2 * orders, rows_own * channels)
-    (waves,) = exchange([synthesis], [synthesis.shape], [(lead, lead)], False, 3)
-    waves = waves.reshape(lon_total, rows_own, channels)
-    grid_back = lax.dot_general(
-        waves,
-        jnp.transpose(basis, (2, 0, 1)).reshape(lon_total, lon_total),
-        (((0,), (0,)), ((), ())),
-        preferred_element_type=jnp.float32,
-    ).astype(jnp.bfloat16)
-    grid_back = jnp.transpose(grid_back, (0, 2, 1))
+    mixed = mixed.reshape(2, degrees, orders, channels)
+    summed = jnp.einsum("klmc,mal->amkc", mixed, legendre, preferred_element_type=jnp.float32)
+    synthesis = (
+        (summed * quadrature[:, None, None, None])
+        .astype(jnp.bfloat16)
+        .reshape(rows_all, 2 * orders, channels)
+    )
+    (waves,) = exchange(
+        [synthesis], [(rows_own, lon_total, channels)], [(by_rows, by_orders)], False, 3
+    )
+    grid_back = jnp.einsum(
+        "apc,pn->anc", waves, waves_of, preferred_element_type=jnp.float32
+    ).astype(jnp.bfloat16)
     (returned_grid,) = exchange(
         [grid_back],
         [stream.shape],
@@ -443,6 +462,7 @@
         jnp.bfloat16
     )
     half = gathered.shape[1] // 2
+    gathered = gathered.astype(jnp.float32)
     grad_expand = gathered[:, :half].reshape(channels, hidden)
     grad_reduce = gathered[:, half:].reshape(channels, hidden).T
     return (grad_input, grad_expand, grad_reduce)

time: 600 us -> 530 us (0.88)
  local copies, waits for them, and re-layouts: 64.2 us -> 30.9 us
  other arithmetic: 22.8 us -> 5.26 us
  Pallas kernels: 463 us -> 447 us
    reshape x8 -> x2, local copies, waits for them, and re-layouts: 32.1 us -> 9.22 us  [the longest x1 4.61 us: direct(): spectrum = blocks.reshape(rows_all, orders, 2, channels)]
    pallas_call x4, Pallas kernels: 225 us -> 209 us  [exchange(): pl.pallas_call(functools.partial(exchange_body, lon_only, views), out_sha...]
    another operation x1 -> x0, other arithmetic: 8.61 us -> none
    select_n x1 -> x0, other arithmetic: 7.35 us -> none  [direct(): jnp.where(arrived, mixed, jnp.zeros_like(mixed))]
    transpose x1 -> x0, local copies, waits for them, and re-layouts: 6.24 us -> none  [direct(): jnp.transpose(basis, (2, 0, 1)).reshape(lon_total, lon_total)]
    convert_element_type x2 -> x1, local copies, waits for them, and re-layouts: 17.9 us -> 14.9 us  [direct(): by_order = jnp.einsum('mal,amkc->klmc', legendre, spectrum, preferred_ele...]
where the time goes in v2:
time: 530 us; the launch traced here: 529 us
  Pallas kernels  447 us (84%)
  matrix products  46 us (9%)
  local copies, waits for them, and re-layouts  30.9 us (6%)
    pallas_call x1, Pallas kernels, mix_exchange(): pl.pallas_call(mix_body, out_shape=[jax.ShapeDtypeStruct(by_order.shape,...  237 us
    pallas_call x4, Pallas kernels, exchange(): pl.pallas_call(functools.partial(exchange_body, lon_only, views), out_sha...  209 us
    convert_element_type x1, local copies, waits for them, and re-layouts, direct(): by_order = jnp.einsum('mal,amkc->klmc', legendre, spectrum, preferred_ele...  14.9 us

profile of v2, /device:TPU:15, one launch (start us, length us, event | category | flops | bytes accessed | tf_op | source)
XLA Modules:
  0.0 529.5 jit_solution(17988296964237514149)
XLA Ops:
  0.7 3.0 fusion.24
  3.7 3.9 fusion.19
  7.6 5.9 %fusion.6 = bf16[4096,512]{1,0:T(8,128)(2,1)S(1)} fusion(f32[4096,512]{1,0:T(8,128)S(1)} %fusion.24, bf16[4096,256]{1,0:T(8,128)(2,1)S(1)} %bitcast.58, bf16[512,256]{1,0:T(8,128)(2,1)S(1)} %copy-done.7), kind=kOutput, calls=%fused_computation.8 | convolution fusion | flops 1113587712 | bytes 14942208 | tf_op jit(solution)/shard_map/dot_general | solution.py:377
  13.5 1.3 fusion.18
  14.8 2.6 fusion.9
  17.4 0.9 pad_maximum_fusion.refs_1_
  18.3 25.9 %shard_map.103 = bf16[4,1024,256]{2,1,0:T(8,128)(2,1)} custom-call(bf16[16,256,256]{2,1,0:T(8,128)(2,1)} %bitcast.54), custom_call_target="tpu_custom_call" | custom-call | tf_op jit(solution)/shard_map/pallas_call | solution.py:199
  44.2 5.9 %convert_bitcast_fusion.2.refs_0_ = bf16[4,1024,256]{2,1,0:T(8,128)(2,1)} fusion(bf16[1024,1024,1]{1,0,2:T(8,128)(2,1)} %constant.19, bf16[4,1024,256]{2,1,0:T(8,128)(2,1)} %shard_map.103), kind=kOutput, calls=%fused_computation.21 | convolution fusion | flops 2148532224 | bytes 6291456 | tf_op jit(solution)/shard_map/pn,anc->apc/dot_general | solution.py:412
  50.1 68.3 %shard_map.104 = (bf16[128,32,256]{2,1,0:T(8,128)(2,1)}, bf16[32,16,512]{2,1,0:T(8,128)(2,1)}) custom-call(bf16[4,1024,256]{2,1,0:T(8,128)(2,1)} %convert_bitcast_fusion.2.refs_0_, bf16[32,16,512]{2,1,0:T(8,128)(2,1)} %pad_maximum_fusion.refs_1_), custom_call_target="tpu_custom_call" | custom-call | tf_op jit(solution)/shard_map/pallas_call | solution.py:199
  118.4 4.6 copy.25
  123.2 7.2 %convert_bitcast_fusion = bf16[2,512,16,256]{1,3,0,2:T(8,128)(2,1)} fusion(bf16[128,16,2,256]{0,3,2,1:T(8,128)(2,1)} %bitcast.56, bf16[16,128,512]{2,1,0:T(8,128)(2,1)S(1)} %copy-done), kind=kOutput, calls=%fused_computation.11 | convolution fusion | flops 1077936128 | bytes 12582912 | tf_op jit(solution)/shard_map/mal,amkc->klmc/dot_general | solution.py:431
  130.3 14.9 %copy.14 = bf16[2,512,16,256]{3,2,1,0:T(8,128)(2,1)} copy(bf16[2,512,16,256]{1,3,0,2:T(8,128)(2,1)} %convert_bitcast_fusion) | data formatting | bytes 16777216 | tf_op jit(solution)/shard_map/convert_element_type | solution.py:432
  145.2 1.6 copy-done.1
  146.8 237.5 %shard_map.105 = (bf16[2,32,16,16,256]{4,3,2,1,0:T(8,128)(2,1)S(1)}, bf16[32,16,512]{2,1,0:T(8,128)(2,1)S(1)}) custom-call(bf16[2,32,16,16,256]{4,3,2,1,0:T(8,128)(2,1)} %bitcast.53, bf16[16,256,256]{2,1,0:T(8,128)(2,1)S(1)} %copy-done.1, bf16[16,512]{1,0:T(8,128)(2,1)S(1)} %multiply_convert_fusion.7.g_ref), custom_call_target="tpu_custom_call" | custom-call | tf_op jit(solution)/shard_map/pallas_call | solution.py:321
  384.3 3.2 copy-done.2
  387.5 10.3 %multiply_convert_fusion.1 = bf16[16,2,256,128]{3,2,1,0:T(8,128)(2,1)} fusion(f32[128]{0:T(128)S(1)} %copy-done.8, bf16[16,128,512]{2,1,0:T(8,128)(2,1)S(1)} %copy-done, bf16[2,512,16,256]{3,2,1,0:T(8,128)(2,1)} %bitcast.52), kind=kOutput, calls=%fused_computation.16 | convolution fusion | flops 1075838976 | bytes 12583424 | tf_op jit(solution)/shard_map/klmc,mal->amkc/dot_general | solution.py:437
  397.8 4.6 copy.26.refs_0_
  402.4 89.5 %shard_map.106 = bf16[4,1024,256]{2,1,0:T(8,128)(2,1)} custom-call(bf16[128,32,256]{2,1,0:T(8,128)(2,1)} %copy.26.refs_0_), custom_call_target="tpu_custom_call" | custom-call | tf_op jit(solution)/shard_map/pallas_call | solution.py:199
  492.0 6.0 %convert_bitcast_fusion.1.refs_0_ = bf16[4,1024,256]{2,1,0:T(8,128)(2,1)} fusion(bf16[4,1024,256]{2,1,0:T(8,128)(2,1)} %shard_map.106, bf16[1024,1024,1]{1,0,2:T(8,128)(2,1)} %constant.19), kind=kOutput, calls=%fused_computation.20 | convolution fusion | flops 2148532224 | bytes 6291456 | tf_op jit(solution)/shard_map/apc,pn->anc/dot_general | solution.py:446
  497.9 25.3 %shard_map.107 = bf16[16,256,256]{2,1,0:T(8,128)(2,1)} custom-call(bf16[4,1024,256]{2,1,0:T(8,128)(2,1)} %convert_bitcast_fusion.1.refs_0_), custom_call_target="tpu_custom_call" | custom-call | tf_op jit(solution)/shard_map/pallas_call | solution.py:199
  523.2 4.2 add_convert_fusion
  527.4 0.1 convert_element_type.70
  527.6 0.9 slice_bitcast_fusion
  528.5 1.0 copy.19
  (18 shorter events, 0.1 us)
Async XLA Ops:
  0.6 122.5 %copy-start = (bf16[16,128,512]{2,1,0:T(8,128)(2,1)S(1)}, bf16[16,128,512]{2,1,0:T(8,128)(2,1)}, u32[]{:S(2)}) copy-start(bf16[16,128,512]{2,1,0:T(8,128)(2,1)} %param.12) | copy-start | bytes 6291460
  0.6 3.0 copy-start.3
  3.7 3.9 copy-start.7
  7.6 5.9 %copy-start.4 = (bf16[16,256,256]{2,1,0:T(8,128)(2,1)S(1)}, bf16[16,256,256]{2,1,0:T(8,128)(2,1)}, u32[]{:S(2)}) copy-start(bf16[16,256,256]{2,1,0:T(8,128)(2,1)} %param.8) | copy-start | bytes 6291460
  13.5 1.3 copy-start.5
  118.4 4.6 copy-start.6
  145.2 1.6 copy-start.1
  146.8 240.7 %copy-start.8 = (f32[128]{0:T(128)S(1)}, f32[128]{0:T(128)}, u32[]{:S(2)}) copy-start(f32[128]{0:T(128)} %param.13) | copy-start | bytes 1540
  384.3 3.2 copy-start.2

commit v3 on v2

--- a/solution.py
+++ b/solution.py
@@ -210,7 +210,7 @@
     )(*arrays)
 
 
-CUTS = 2
+CUTS = 4
 
 
 def mix_body(

time: 530 us -> 519 us (0.979)
  Pallas kernels: 447 us -> 435 us
    pallas_call x4, Pallas kernels: 209 us -> 189 us  [exchange(): pl.pallas_call(functools.partial(exchange_body, lon_only, views), out_sha...]
    pallas_call x1, Pallas kernels: 237 us -> 247 us  [mix_exchange(): pl.pallas_call(mix_body, out_shape=[jax.ShapeDtypeStruct(by_order.shape,...]
where the time goes in v3:
time: 519 us; the launch traced here: 518 us
  Pallas kernels  435 us (84%)
  matrix products  46 us (9%)
  local copies, waits for them, and re-layouts  30.9 us (6%)
  other arithmetic  5.26 us (1%)
    pallas_call x1, Pallas kernels, mix_exchange(): pl.pallas_call(mix_body, out_shape=[jax.ShapeDtypeStruct(by_order.shape,...  247 us
    pallas_call x4, Pallas kernels, exchange(): pl.pallas_call(functools.partial(exchange_body, lon_only, views), out_sha...  189 us
    convert_element_type x1, local copies, waits for them, and re-layouts, direct(): by_order = jnp.einsum('mal,amkc->klmc', legendre, spectrum, preferred_ele...  14.9 us

profile of v3, /device:TPU:15, one launch (start us, length us, event | category | flops | bytes accessed | tf_op | source)
XLA Modules:
  0.0 518.4 jit_solution(11086639691188946945)
XLA Ops:
  0.7 3.0 fusion.24
  3.7 3.9 fusion.19
  7.6 5.9 %fusion.6 = bf16[4096,512]{1,0:T(8,128)(2,1)S(1)} fusion(f32[4096,512]{1,0:T(8,128)S(1)} %fusion.24, bf16[4096,256]{1,0:T(8,128)(2,1)S(1)} %bitcast.58, bf16[512,256]{1,0:T(8,128)(2,1)S(1)} %copy-done.7), kind=kOutput, calls=%fused_computation.8 | convolution fusion | flops 1113587712 | bytes 14942208 | tf_op jit(solution)/shard_map/dot_general | solution.py:377
  13.5 1.3 fusion.18
  14.8 2.6 fusion.9
  17.4 0.9 pad_maximum_fusion.refs_1_
  18.3 25.9 %shard_map.103 = bf16[4,1024,256]{2,1,0:T(8,128)(2,1)} custom-call(bf16[16,256,256]{2,1,0:T(8,128)(2,1)} %bitcast.54), custom_call_target="tpu_custom_call" | custom-call | tf_op jit(solution)/shard_map/pallas_call | solution.py:199
  44.2 5.9 %convert_bitcast_fusion.2.refs_0_ = bf16[4,1024,256]{2,1,0:T(8,128)(2,1)} fusion(bf16[1024,1024,1]{1,0,2:T(8,128)(2,1)} %constant.19, bf16[4,1024,256]{2,1,0:T(8,128)(2,1)} %shard_map.103), kind=kOutput, calls=%fused_computation.21 | convolution fusion | flops 2148532224 | bytes 6291456 | tf_op jit(solution)/shard_map/pn,anc->apc/dot_general | solution.py:412
  50.1 68.3 %shard_map.104 = (bf16[128,32,256]{2,1,0:T(8,128)(2,1)}, bf16[32,16,512]{2,1,0:T(8,128)(2,1)}) custom-call(bf16[4,1024,256]{2,1,0:T(8,128)(2,1)} %convert_bitcast_fusion.2.refs_0_, bf16[32,16,512]{2,1,0:T(8,128)(2,1)} %pad_maximum_fusion.refs_1_), custom_call_target="tpu_custom_call" | custom-call | tf_op jit(solution)/shard_map/pallas_call | solution.py:199
  118.4 4.6 copy.25
  123.2 7.2 %convert_bitcast_fusion = bf16[2,512,16,256]{1,3,0,2:T(8,128)(2,1)} fusion(bf16[128,16,2,256]{0,3,2,1:T(8,128)(2,1)} %bitcast.56, bf16[16,128,512]{2,1,0:T(8,128)(2,1)S(1)} %copy-done), kind=kOutput, calls=%fused_computation.11 | convolution fusion | flops 1077936128 | bytes 12582912 | tf_op jit(solution)/shard_map/mal,amkc->klmc/dot_general | solution.py:431
  130.3 14.9 %copy.14 = bf16[2,512,16,256]{3,2,1,0:T(8,128)(2,1)} copy(bf16[2,512,16,256]{1,3,0,2:T(8,128)(2,1)} %convert_bitcast_fusion) | data formatting | bytes 16777216 | tf_op jit(solution)/shard_map/convert_element_type | solution.py:432
  145.2 1.6 copy-done.1
  146.8 246.7 %shard_map.105 = (bf16[2,32,16,16,256]{4,3,2,1,0:T(8,128)(2,1)S(1)}, bf16[32,16,512]{2,1,0:T(8,128)(2,1)S(1)}) custom-call(bf16[2,32,16,16,256]{4,3,2,1,0:T(8,128)(2,1)} %bitcast.53, bf16[16,256,256]{2,1,0:T(8,128)(2,1)S(1)} %copy-done.1, bf16[16,512]{1,0:T(8,128)(2,1)S(1)} %multiply_convert_fusion.7.g_ref), custom_call_target="tpu_custom_call" | custom-call | tf_op jit(solution)/shard_map/pallas_call | solution.py:321
  393.6 3.2 copy-done.2
  396.8 10.3 %multiply_convert_fusion.1 = bf16[16,2,256,128]{3,2,1,0:T(8,128)(2,1)} fusion(f32[128]{0:T(128)S(1)} %copy-done.8, bf16[16,128,512]{2,1,0:T(8,128)(2,1)S(1)} %copy-done, bf16[2,512,16,256]{3,2,1,0:T(8,128)(2,1)} %bitcast.52), kind=kOutput, calls=%fused_computation.16 | convolution fusion | flops 1075838976 | bytes 12583424 | tf_op jit(solution)/shard_map/klmc,mal->amkc/dot_general | solution.py:437
  407.1 4.6 copy.26.refs_0_
  411.7 69.2 %shard_map.106 = bf16[4,1024,256]{2,1,0:T(8,128)(2,1)} custom-call(bf16[128,32,256]{2,1,0:T(8,128)(2,1)} %copy.26.refs_0_), custom_call_target="tpu_custom_call" | custom-call | tf_op jit(solution)/shard_map/pallas_call | solution.py:199
  480.9 6.0 %convert_bitcast_fusion.1.refs_0_ = bf16[4,1024,256]{2,1,0:T(8,128)(2,1)} fusion(bf16[4,1024,256]{2,1,0:T(8,128)(2,1)} %shard_map.106, bf16[1024,1024,1]{1,0,2:T(8,128)(2,1)} %constant.19), kind=kOutput, calls=%fused_computation.20 | convolution fusion | flops 2148532224 | bytes 6291456 | tf_op jit(solution)/shard_map/apc,pn->anc/dot_general | solution.py:446
  486.8 25.3 %shard_map.107 = bf16[16,256,256]{2,1,0:T(8,128)(2,1)} custom-call(bf16[4,1024,256]{2,1,0:T(8,128)(2,1)} %convert_bitcast_fusion.1.refs_0_), custom_call_target="tpu_custom_call" | custom-call | tf_op jit(solution)/shard_map/pallas_call | solution.py:199
  512.2 4.2 add_convert_fusion
  516.4 0.1 convert_element_type.70
  516.5 0.9 slice_bitcast_fusion
  517.4 1.0 copy.19
  (18 shorter events, 0.1 us)
Async XLA Ops:
  0.6 122.5 %copy-start = (bf16[16,128,512]{2,1,0:T(8,128)(2,1)S(1)}, bf16[16,128,512]{2,1,0:T(8,128)(2,1)}, u32[]{:S(2)}) copy-start(bf16[16,128,512]{2,1,0:T(8,128)(2,1)} %param.12) | copy-start | bytes 6291460
  0.6 3.0 copy-start.3
  3.7 3.9 copy-start.7
  7.6 5.9 %copy-start.4 = (bf16[16,256,256]{2,1,0:T(8,128)(2,1)S(1)}, bf16[16,256,256]{2,1,0:T(8,128)(2,1)}, u32[]{:S(2)}) copy-start(bf16[16,256,256]{2,1,0:T(8,128)(2,1)} %param.8) | copy-start | bytes 6291460
  13.5 1.3 copy-start.5
  118.4 4.6 copy-start.6
  145.2 1.6 copy-start.1
  146.8 250.0 %copy-start.8 = (f32[128]{0:T(128)S(1)}, f32[128]{0:T(128)}, u32[]{:S(2)}) copy-start(f32[128]{0:T(128)} %param.13) | copy-start | bytes 1540
  393.6 3.2 copy-start.2
